TPU v7x, 256 devices: a whole 4x4x8 slice. The times are simulated.
256 devices in a mesh: ctx: 64 (over z, y, core), tp: 4 (over x).
Axes of the slice: x: 4, y: 4, z: 8, core: 2. Of those that a mesh axis runs over, the one named last changes fastest.
Arguments:
- hidden: bfloat16 [8192, 5120], P('ctx'), may hold values from -12 to 12, as said below
- w_query: bfloat16 [5120, 2560], P('ctx', 'tp'), may hold values from -0.078125 to 0.078125
- w_keyval: bfloat16 [5120, 4, 256], P('ctx', 'tp'), may hold values from -0.078125 to 0.078125
- w_out: bfloat16 [2560, 5120], P('tp', 'ctx'), may hold values from -0.125 to 0.125
- episode_lengths: int32 [16], replicated, may hold values from 1 to 4096, 8192 in all
Outputs:
- attended: bfloat16 [8192, 5120], P('ctx', 'tp')
Inputs may be any that keep to these rules, and one draw needn't show every extreme that they name: `hidden`: each row's entries are real numbers; no further structure is promised.
All inputs are finite; a program needn't handle non-finite values.
Results may differ from a plain program's by a relative error of at most 0.015.
The roundings to bfloat16 on the way count: a program that leaves them out, or rounds other values in their place, can miss the bound.
Values may be sent and summed in bfloat16 or wider, within the bound.
A program may use at most 64 MiB of HBM per device.

v0:
```python
import jax
import jax.numpy as jnp
from jax import lax
from jax.sharding import PartitionSpec as P


def rotate(values_in, positions):
    half_dim = values_in.shape[-1] // 2
    freqs = 1000000.0 ** (-(jnp.arange(half_dim, dtype=jnp.float32) * 2.0) / values_in.shape[-1])
    angles = positions.astype(jnp.float32)[:, None] * freqs[None, :]
    cosine = jnp.cos(angles)[:, None, :]
    sine = jnp.sin(angles)[:, None, :]
    first_half = values_in[..., :half_dim]
    second_half = values_in[..., half_dim:]
    return jnp.concatenate(
        [first_half * cosine - second_half * sine, second_half * cosine + first_half * sine],
        axis=-1,
    )


def first_of(tokens_at, episode_ends):
    return jnp.max(
        jnp.where(episode_ends[None, :] <= tokens_at[:, None], episode_ends[None, :], 0), axis=1
    )


def local(hidden, w_query, w_keyval, w_out, episode_lengths):
    tok_rows = hidden.shape[0]
    ctx_index = lax.axis_index("ctx")
    key_heads = w_keyval.shape[1]
    head_size = w_keyval.shape[2] // 2
    query_heads = w_query.shape[1] // head_size
    group = query_heads // key_heads
    score_scale = 1.0 / head_size**0.5
    pieces = (
        lax.all_gather(w_query, "ctx", axis=0, tiled=True),
        lax.all_gather(w_keyval, "ctx", axis=0, tiled=True),
    )
    query_sum = jnp.dot(hidden, pieces[0], preferred_element_type=jnp.float32)
    keyval_sum = jnp.dot(
        hidden, pieces[1].reshape(pieces[1].shape[0], -1), preferred_element_type=jnp.float32
    )
    query_sum, keyval_sum = (query_sum, keyval_sum)
    tokens_at = ctx_index * tok_rows + jnp.arange(tok_rows, dtype=jnp.int32)
    episode_ends = jnp.cumsum(episode_lengths)
    firsts = first_of(tokens_at, episode_ends)
    positions = tokens_at - firsts
    q_rot = rotate(query_sum.reshape(tok_rows, query_heads, head_size), positions).astype(
        jnp.bfloat16
    )
    keyval = keyval_sum.reshape(tok_rows, key_heads, 2, head_size)
    k_rot = rotate(keyval[:, :, 0], positions).astype(jnp.bfloat16)
    v_local = keyval[:, :, 1].astype(jnp.bfloat16)
    grouped = q_rot.reshape(tok_rows, key_heads, group, head_size)

    def attend_block(running, key_rows, value_rows, key_first):
        run_max, run_sum, run_acc = running
        scores = (
            jnp.einsum("qhgd,khd->hgqk", grouped, key_rows, preferred_element_type=jnp.float32)
            * score_scale
        )
        key_at = key_first + jnp.arange(key_rows.shape[0], dtype=jnp.int32)
        allowed = (key_at[None, :] >= firsts[:, None]) & (key_at[None, :] <= tokens_at[:, None])
        scores = jnp.where(allowed, scores, -1e30)
        new_max = jnp.maximum(run_max, jnp.max(scores, axis=-1))
        factor = jnp.exp(run_max - new_max)
        weights_exp = jnp.where(allowed, jnp.exp(scores - new_max[..., None]), 0.0)
        new_sum = run_sum * factor + jnp.sum(weights_exp, axis=-1)
        new_acc = run_acc * factor[..., None] + jnp.einsum(
            "hgqk,khd->hgqd",
            weights_exp.astype(jnp.bfloat16),
            value_rows,
            preferred_element_type=jnp.float32,
        )
        return (new_max, new_sum, new_acc)

    empty = (
        jnp.full((key_heads, group, tok_rows), -1e30, jnp.float32),
        jnp.zeros((key_heads, group, tok_rows), jnp.float32),
        jnp.zeros((key_heads, group, tok_rows, head_size), jnp.float32),
    )
    pieces = (
        lax.all_gather(k_rot, "ctx", axis=0, tiled=True),
        lax.all_gather(v_local, "ctx", axis=0, tiled=True),
    )
    key_rows = pieces[0]
    count = key_rows.shape[0]
    blocks = count // tok_rows
    key_blocks = key_rows.reshape(blocks, tok_rows, key_heads, head_size)
    value_blocks = pieces[1].reshape(blocks, tok_rows, key_heads, head_size)
    block_firsts = jnp.arange(blocks, dtype=jnp.int32) * tok_rows

    def scan_step(state, items):
        return (attend_block(state, items[0], items[1], items[2]), None)

    result, unused = lax.scan(scan_step, empty, (key_blocks, value_blocks, block_firsts))
    run_max, run_sum, run_acc = result
    mixed = run_acc / run_sum[..., None]
    context = (
        jnp.transpose(mixed, (2, 0, 1, 3))
        .reshape(tok_rows, query_heads * head_size)
        .astype(jnp.bfloat16)
    )
    terms = jnp.dot(
        context,
        lax.all_gather(w_out, "ctx", axis=1, tiled=True),
        preferred_element_type=jnp.float32,
    )
    return lax.psum_scatter(terms.astype(jnp.bfloat16), "tp", scatter_dimension=1, tiled=True)


def solution(mesh):
    placed = (P("ctx", None), P("ctx", "tp"), P("ctx", "tp", None), P("tp", "ctx"), P())
    return jax.shard_map(
        local, mesh=mesh, in_specs=placed, out_specs=P("ctx", "tp"), check_vma=False
    )
```

profile of v0, /device:TPU:1, one launch (start us, length us, event | category | flops | bytes accessed | tf_op | source)
XLA Modules:
  0.0 595.8 jit_solution(15326421800488307082)
XLA Ops:
  8.3 83.8 %all-gather.7.cloned.1.call-done = bf16[5120,1,256]{2,0,1:T(8,128)(2,1)} async-done(((bf16[80,1,256]{2,0,1:T(8,128)(2,1)}), bf16[5120,1,256]{2,0,1:T(8,128)(2,1)}) %all-gather.7.cloned.1.call-update) | async-done | bytes 2621456 | tf_op jit(solution)/shard_map/all_gather | solution.py:37
  92.1 4.4 copy.23
  96.6 2.6 fusion.23
  102.2 68.0 %all-gather.9.cloned.1.call-done = bf16[8192,1,128]{0,2,1:T(8,128)(2,1)} async-done(((bf16[128,1,128]{0,2,1:T(8,128)(2,1)}), bf16[8192,1,128]{0,2,1:T(8,128)(2,1)}) %all-gather.9.cloned.1.call-update) | async-done | bytes 2097168 | tf_op jit(solution)/shard_map/all_gather | solution.py:83
  170.2 4.1 copy.31
  174.3 70.0 %all-gather.15.cloned.1.call-done = bf16[8192,1,1,128]{0,3,2,1:T(8,128)(2,1)} async-done(((bf16[128,1,1,128]{0,3,2,1:T(8,128)(2,1)}), bf16[8192,1,1,128]{0,3,2,1:T(8,128)(2,1)}) %all-gather.15.cloned.1.call-update) | async-done | bytes 2097168 | tf_op jit(solution)/shard_map/all_gather | solution.py:84
  244.2 4.1 copy.32
  248.3 78.9 %all-gather.11.cloned.1.call-done = bf16[5120,640]{1,0:T(8,128)(2,1)} async-done(((bf16[80,640]{1,0:T(8,128)(2,1)}), bf16[5120,640]{1,0:T(8,128)(2,1)}) %all-gather.11.cloned.1.call-update) | async-done | bytes 6553616 | tf_op jit(solution)/shard_map/all_gather | solution.py:36
  327.2 5.5 fusion.37
  333.0 227.5 %while.15 = (s32[]{:T(128)}, f32[1,5,128]{2,1,0:T(8,128)S(1)}, f32[1,5,128]{2,1,0:T(8,128)S(1)}, f32[1,5,128,128]{3,2,1,0:T(8,128)S(1)}, s32[64]{0:T(128)S(1)}, ...) while((s32[]{:T(128)}, f32[1,5,128]{2,1,0:T(8,128)S(1)}, ...), condition=%wide.region_5.6_spmd.clone, body=%wide.region_2.5_spmd.clone.sunk | while | flops 42979328 | bytes 1978005 | solution.py:96
  335.3 1.1 fusion.54
  338.9 1.1 fusion.54
  342.4 1.1 fusion.54
  346.0 1.1 fusion.54
  349.5 1.1 fusion.54
  353.1 1.1 fusion.54
  356.6 1.1 fusion.54
  360.2 1.1 fusion.54
  363.8 1.1 fusion.54
  367.3 1.1 fusion.54
  370.9 1.1 fusion.54
  374.4 1.1 fusion.54
  378.0 1.1 fusion.54
  381.5 1.1 fusion.54
  385.1 1.1 fusion.54
  388.6 1.1 fusion.54
  392.2 1.1 fusion.54
  395.8 1.1 fusion.54
  399.3 1.1 fusion.54
  402.9 1.1 fusion.54
  406.5 1.1 fusion.54
  410.0 1.1 fusion.54
  413.6 1.1 fusion.54
  417.1 1.1 fusion.54
  420.7 1.1 fusion.54
  424.2 1.1 fusion.54
  427.8 1.1 fusion.54
  431.3 1.1 fusion.54
  434.9 1.1 fusion.54
  438.4 1.1 fusion.54
  442.0 1.1 fusion.54
  445.6 1.1 fusion.54
  449.1 1.1 fusion.54
  452.7 1.1 fusion.54
  456.2 1.1 fusion.54
  459.8 1.1 fusion.54
  463.3 1.1 fusion.54
  466.9 1.1 fusion.54
  470.4 1.1 fusion.54
  474.0 1.1 fusion.54
  477.5 1.1 fusion.54
  481.1 1.1 fusion.54
  484.6 1.1 fusion.54
  488.2 1.1 fusion.54
  491.8 1.1 fusion.54
  495.3 1.1 fusion.54
  498.9 1.1 fusion.54
  502.4 1.1 fusion.54
  506.0 1.1 fusion.54
  509.5 1.1 fusion.54
  513.1 1.1 fusion.54
  545.1 1.1 fusion.54
  560.7 6.2 %convolution_convert_fusion = bf16[128,5120]{1,0:T(8,128)(2,1)} fusion(bf16[128,640]{0,1:T(8,128)(2,1)S(1)} %bitcast.94, bf16[640,5120]{0,1:T(8,128)(2,1)} %all-gather.13.cloned.1.call-done), kind=kOutput, calls=%fused_computation.30 | convolution fusion | flops 839516160 | bytes 8028160 | tf_op jit(solution)/shard_map/dot_general | solution.py:104
  566.9 22.1 %reduce-scatter.2.cloned.1.call-done = bf16[128,1280]{1,0:T(8,128)(2,1)} async-done(((bf16[128,5120]{1,0:T(8,128)(2,1)}), bf16[128,1280]{1,0:T(8,128)(2,1)}) %reduce-scatter.2.cloned.1.call-update) | async-done | bytes 327696 | tf_op jit(solution)/shard_map/reduce_scatter | solution.py:109
  (560 shorter events, 171.7 us)
Async XLA Ops:
  6.5 90.0 %copy-start = (bf16[128,5120]{1,0:T(8,128)(2,1)S(1)}, bf16[128,5120]{1,0:T(8,128)(2,1)}, u32[]{:S(2)}) copy-start(bf16[128,5120]{1,0:T(8,128)(2,1)} %param.7) | copy-start | bytes 3932164
  6.5 85.6 %all-gather.7.cloned.1.call-start = ((), (), s32[]{:S(2)}) async-start(), calls=%async_computation.1 | async-start | bytes 2662400 | tf_op jit(solution)/shard_map/all_gather | solution.py:37
  7.3 162.9 %all-gather.9.cloned.1.call-start = ((), (), s32[]{:S(2)}) async-start(), calls=%async_computation.2 | async-start | bytes 2129920 | tf_op jit(solution)/shard_map/all_gather | solution.py:83
  100.0 144.2 %all-gather.15.cloned.1.call-start = ((), (), s32[]{:S(2)}) async-start(), calls=%async_computation.6 | async-start | bytes 2129920 | tf_op jit(solution)/shard_map/all_gather | solution.py:84
  100.7 226.5 %all-gather.11.cloned.1.call-start = ((), (), s32[]{:S(2)}) async-start(), calls=%async_computation.3 | async-start | bytes 6656000 | tf_op jit(solution)/shard_map/all_gather | solution.py:36
  101.3 459.4 %all-gather.13.cloned.1.call-start = ((), (), s32[]{:S(2)}) async-start(), calls=%async_computation.4 | async-start | bytes 6656000 | tf_op jit(solution)/shard_map/all_gather | solution.py:106
  101.9 487.1 %reduce-scatter.2.cloned.1.call-start = ((), (), s32[]{:S(2)}) async-start(), calls=%async_computation.5 | async-start | bytes 1638400 | tf_op jit(solution)/shard_map/reduce_scatter | solution.py:109
Sparse Core Ops, SparseCore 0:
  10.1 81.9 all-gather.6
  100.1 70.0 all-gather.8
  172.8 71.3 all-gather.14
  246.8 80.3 all-gather.10
  329.7 78.0 all-gather.12
  567.0 21.9 reduce-scatter.1
where the time goes:
time: 606 us; the launch traced here: 596 us
  waiting for transfers between devices  325 us (54%)
  matrix products  147 us (24%)
  other arithmetic  54.2 us (9%)
  local copies, waits for them, and re-layouts  52 us (9%)
  between operations  13.6 us (2%)
    all_gather x1, waiting for transfers between devices, local(): lax.all_gather(w_keyval, 'ctx', axis=0, tiled=True)  83.8 us
    all_gather x1, waiting for transfers between devices, local(): lax.all_gather(w_query, 'ctx', axis=0, tiled=True)  78.9 us
    all_gather x1, waiting for transfers between devices, local(): lax.all_gather(v_local, 'ctx', axis=0, tiled=True)  70 us
    dot_general x64, matrix products, attend_block(): jnp.einsum('hgqk,khd->hgqd', weights_exp.astype(jnp.bfloat16), value_rows...  69.7 us
    all_gather x1, waiting for transfers between devices, local(): lax.all_gather(k_rot, 'ctx', axis=0, tiled=True)  68 us
    dot_general x64, matrix products, attend_block(): jnp.einsum('qhgd,khd->hgqk', grouped, key_rows, preferred_element_type=jn...  63 us
    add x65, other arithmetic, local(): tokens_at = ctx_index * tok_rows + jnp.arange(tok_rows, dtype=jnp.int32)  41.4 us
    dynamic_slice x64, local copies, waits for them, and re-layouts, local(): lax.scan(scan_step, empty, (key_blocks, value_blocks, block_firsts))  37.5 us
  transfers between devices with their start and end apart: 6, of which 5 were waited for; matrix products, arithmetic and copies ran while one was open for 40% of the time, Pallas kernels for 0%

commit v1 on v0

v1 whole, which is shorter than its diff:
```python
import functools
import math

import jax
import jax.numpy as jnp
import numpy as np
from jax import lax
from jax.experimental import pallas as pl
from jax.experimental.pallas import tpu as pltpu
from jax.sharding import PartitionSpec as P

MESH = pl.DeviceIdType.MESH
NZ, NY, NX = 8, 4, 4
ROWS = 128
HEADS = 5
HD = 128
NEG = -1e30
F32 = jnp.float32
BF = jnp.bfloat16


class Place:
    def __init__(self):
        index = lax.axis_index("ctx")
        self.index = index
        self.z = index // (2 * NY)
        self.y = lax.rem(index // 2, NY)
        self.c = lax.rem(index, 2)
        self.x = lax.axis_index("tp")

    def zof(self, dz):
        return lax.rem(self.z + (dz + NZ), NZ)

    def yof(self, dy):
        return lax.rem(self.y + (dy + NY), NY)

    def xof(self, dx):
        return lax.rem(self.x + (dx + NX), NX)

    def dev(self, dz=0, dy=0, dc=0, dx=0):
        c = 1 - self.c if dc else self.c
        return ((self.zof(dz) * NY + self.yof(dy)) * 2 + c, self.xof(dx))


def rcopy(src, dst, ssem, rsem, dev):
    return pltpu.make_async_remote_copy(
        src_ref=src, dst_ref=dst, send_sem=ssem, recv_sem=rsem, device_id=dev, device_id_type=MESH
    )


class Gather:
    def __init__(self, place, own, block, slab, sems, sign):
        self.p = place
        self.own = own
        self.block = block
        self.slab = slab
        self.zs, self.zr, self.ys, self.yr = sems
        self.sign = sign

    def zslot(self, r):
        if r <= 4:
            return self.p.zof(-self.sign * r)
        return self.p.zof(self.sign * (r - 4))

    def zcopy(self, core, hop, right):
        r = hop if right else (hop + 4 if hop else 0)
        z = self.zslot(r)
        dst = self.block(z, self.p.y) if core == 0 else self.slab(z)
        src = dst
        i = hop if right else 4 + hop
        j = hop + 1 if right else 5 + hop
        return rcopy(
            src, dst, self.zs.at[i], self.zr.at[j], self.p.dev(dz=self.sign if right else -self.sign)
        )

    def zwait(self, core, r):
        z = self.zslot(r)
        dst = self.block(z, self.p.y) if core == 0 else self.slab(z)
        rcopy(dst, dst, self.zs.at[0], self.zr.at[r], self.p.dev(dz=1)).wait_recv()

    def ycopy(self, r, k):
        ref = self.block(self.zslot(r), self.p.y)
        i = r * 3 + k - 1
        return rcopy(ref, ref, self.ys.at[i], self.yr.at[i], self.p.dev(dy=k))

    def ysend(self, r):
        for k in (1, 3, 2):
            self.ycopy(r, k).start()

    def ywait(self, r):
        for k in (1, 3, 2):
            i = r * 3 + k - 1
            ref = self.block(self.zslot(r), self.p.yof(-k))
            rcopy(ref, ref, self.ys.at[i], self.yr.at[i], self.p.dev(dy=k)).wait_recv()

    def start(self):
        @pl.when(self.p.c == 0)
        def _():
            self.zcopy(0, 0, True).start()
            self.zcopy(0, 0, False).start()

        self.ysend(0)

    def mid(self):
        self.ywait(0)

        @pl.when(self.p.c == 1)
        def _():
            self.zcopy(1, 0, True).start()
            self.zcopy(1, 0, False).start()

    def hop(self, s):
        for core in (0, 1):

            @pl.when(self.p.c == core)
            def _(core=core):
                self.zwait(core, s)
                if s < 4:
                    self.zcopy(core, s, True).start()
                    self.zwait(core, 4 + s)
                if s < 3:
                    self.zcopy(core, s, False).start()
                if core == 0:
                    self.ysend(s)
                    if s < 4:
                        self.ysend(4 + s)

    def ready(self, r):
        if r == 0:
            return

        @pl.when(self.p.c == 0)
        def _():
            self.ywait(r)

    def drain(self):
        for core in (0, 1):

            @pl.when(self.p.c == core)
            def _(core=core):
                for hop in range(4):
                    self.zcopy(core, hop, True).wait_send()
                for hop in range(3):
                    self.zcopy(core, hop, False).wait_send()
                for r in range(8) if core == 0 else (0,):
                    for k in (1, 2, 3):
                        self.ycopy(r, k).wait_send()


def kernel(
    lens, hid, wq, wkv, wot, freq, out,
    hh, wqb, wkvb, wob, kvb, acc_kv, acc_q, p_kv, p_q, qb, tok_first, cos_t, sin_t,
    m_s, l_s, a_s, ctx_t, xs, xr, x_own, f_send, f_recv, fin,
    *sems,
):
    p = Place()
    z, y, c, x = p.z, p.y, p.c, p.x
    a_sems, b_sems, d_sems = sems[0:4], sems[4:8], sems[8:12]
    c_zs, c_zr, c_ys, c_yr, c_ss, c_sr = sems[12:18]
    misc_s, misc_r, x_ss, x_sr = sems[18:22]

    barrier = pltpu.get_barrier_semaphore()
    peers = [dict(dz=1), dict(dz=-1), dict(dy=1), dict(dy=2), dict(dy=3), dict(dc=1), dict(dx=1), dict(dx=2), dict(dx=3)]
    for d in peers:
        pl.semaphore_signal(barrier, inc=1, device_id=p.dev(**d), device_id_type=MESH)

    wkvb[z, y, c] = wkv[...]
    wqb[z, y, c] = wq[...]
    wob[z, y] = wot[...]

    def clear(i, carry):
        wkvb[i // NY, lax.rem(i, NY), 1 - c] = jnp.zeros((80, 256), BF)
        wqb[i // NY, lax.rem(i, NY), 1 - c] = jnp.zeros((80, 640), BF)
        return carry

    lax.fori_loop(0, NZ * NY, clear, 0)
    hh[c] = hid[...]

    pl.semaphore_wait(barrier, len(peers))

    gather_a = Gather(
        p, wkv, lambda zz, yy: wkvb.at[zz, yy, c], lambda zz: wkvb.at[zz, :, c], a_sems, 1
    )
    gather_b = Gather(
        p, wq, lambda zz, yy: wqb.at[zz, yy, c], lambda zz: wqb.at[zz, :, c], b_sems, -1
    )
    gather_d = Gather(p, wot, lambda zz, yy: wob.at[zz, yy], lambda zz: wob.at[zz], d_sems, 1)

    def sibling(i, src, dst):
        return rcopy(src, dst, misc_s.at[i], misc_r.at[i], p.dev(dc=1))

    gather_a.start()
    hid_copy = sibling(0, hh.at[c], hh.at[c])
    hid_copy.start()
    gather_b.start()

    tok = p.index * ROWS + lax.broadcasted_iota(jnp.int32, (ROWS, HD), 0)
    first = jnp.zeros((ROWS, HD), jnp.int32)
    end = jnp.int32(0)
    for i in range(16):
        end = end + lens[i]
        first = jnp.maximum(first, jnp.where(end <= tok, end, 0))
    tok_first[...] = first
    angle = (tok - first).astype(F32) * freq[...]
    cos_t[...] = jnp.cos(angle)
    lane = lax.broadcasted_iota(jnp.int32, (ROWS, HD), 1)
    sine = jnp.sin(angle)
    sin_t[...] = jnp.where(lane < HD // 2, -sine, sine)

    def rotate(v):
        return v * cos_t[...] + pltpu.roll(v, HD // 2, 1) * sin_t[...]

    def project(gather, buf, acc, r, width, init=False):
        gather.ready(r)
        zz = gather.zslot(r)
        left = hh[:, :, pl.ds(pl.multiple_of(zz * 640, 128), 640)].reshape(2 * ROWS, 640)
        right = buf[zz].reshape(640, width)
        term = jnp.dot(left, right, preferred_element_type=F32).reshape(2, ROWS, width)
        if init:
            acc[...] = term
        else:
            acc[...] += term

    proj_a = functools.partial(project, gather_a, wkvb, acc_kv, width=256)
    proj_b = functools.partial(project, gather_b, wqb, acc_q, width=640)

    gather_a.mid()
    gather_a.hop(1)
    gather_b.mid()
    hid_copy.wait_recv()
    proj_a(r=0, init=True)
    gather_a.hop(2)
    proj_a(r=1)
    proj_a(r=5)
    gather_a.hop(3)
    proj_a(r=2)
    proj_a(r=6)
    gather_b.hop(1)
    gather_a.hop(4)
    proj_a(r=3)
    proj_a(r=7)
    proj_a(r=4)
    kv_copy = sibling(1, acc_kv.at[1 - c], p_kv)
    kv_copy.start()
    proj_b(r=0, init=True)
    kv_copy.wait_recv()
    keyval = acc_kv[c] + p_kv[...]
    kvb[z, c, y] = jnp.concatenate(
        [rotate(keyval[:, :HD]).astype(BF), keyval[:, HD:].astype(BF)], axis=1
    )

    def c_block(s, dy=0):
        return kvb.at[p.zof(-s), c, p.yof(dy)]

    def c_z(s):
        return rcopy(c_block(s), c_block(s), c_zs.at[s], c_zr.at[s + 1], p.dev(dz=1))

    def c_y(s, k):
        i = s * 3 + k - 1
        return rcopy(c_block(s), c_block(s), c_ys.at[i], c_yr.at[i], p.dev(dy=k))

    def c_sib(s):
        ref = kvb.at[p.zof(-s), c]
        return rcopy(ref, ref, c_ss.at[s], c_sr.at[s], p.dev(dc=1))

    def c_hop(s):
        if s:
            rcopy(c_block(s), c_block(s), c_zs.at[0], c_zr.at[s], p.dev(dz=1)).wait_recv()
        if s < 4:
            c_z(s).start()
        for k in (1, 3, 2):
            c_y(s, k).start()

    def c_plane(s):
        for k in (1, 3, 2):
            i = s * 3 + k - 1
            rcopy(c_block(s, -k), c_block(s, -k), c_ys.at[i], c_yr.at[i], p.dev(dy=k)).wait_recv()
        c_sib(s).start()

    def c_other(s):
        ref = kvb.at[p.zof(-s), 1 - c]
        rcopy(ref, ref, c_ss.at[s], c_sr.at[s], p.dev(dc=1)).wait_recv()

    c_hop(0)
    gather_b.hop(2)
    proj_b(r=1)
    proj_b(r=5)
    c_hop(1)
    c_plane(0)
    gather_b.hop(3)
    gather_d.start()
    proj_b(r=2)
    proj_b(r=6)
    c_hop(2)
    c_plane(1)
    gather_b.hop(4)
    proj_b(r=3)
    proj_b(r=7)
    c_hop(3)
    c_plane(2)
    gather_d.mid()
    proj_b(r=4)
    q_copy = sibling(2, acc_q.at[1 - c], p_q)
    q_copy.start()
    c_hop(4)
    c_plane(3)
    q_copy.wait_recv()
    query = acc_q[c] + p_q[...]
    for h in range(HEADS):
        qb[h] = rotate(query[:, h * HD : (h + 1) * HD]).astype(BF)
    gather_d.hop(1)

    scale = math.log2(math.e) / math.sqrt(HD)
    spot = lax.broadcasted_iota(jnp.int32, (ROWS, 4 * HD), 1)
    spot = (spot // ROWS) * (2 * ROWS) + lax.rem(spot, ROWS)
    wide_tok = p.index * ROWS + lax.broadcasted_iota(jnp.int32, (ROWS, 4 * HD), 0)

    def chunk(s, core, init=False):
        zp = p.zof(-s)
        key_at = spot + (zp * (2 * NY * ROWS) + core * ROWS)
        wide_first = jnp.concatenate([tok_first[...]] * 4, axis=1)
        bias = jnp.where((key_at >= wide_first) & (key_at <= wide_tok), 0.0, NEG)
        keys = kvb[zp, core, :, :, 0:HD].reshape(4 * ROWS, HD)
        values = kvb[zp, core, :, :, HD : 2 * HD].reshape(4 * ROWS, HD)
        for h in range(HEADS):
            score = lax.dot_general(
                qb[h], keys, (((1,), (1,)), ((), ())), preferred_element_type=F32
            )
            score = score * scale + bias
            top = jnp.broadcast_to(jnp.max(score, axis=1, keepdims=True), (ROWS, HD))
            if not init:
                old = m_s[h]
                top = jnp.maximum(old, top)
            weight = jnp.exp2(score - jnp.concatenate([top] * 4, axis=1))
            part = (weight[:, :HD] + weight[:, HD : 2 * HD]) + (
                weight[:, 2 * HD : 3 * HD] + weight[:, 3 * HD :]
            )
            mixed = jnp.dot(weight.astype(BF), values, preferred_element_type=F32)
            m_s[h] = top
            if init:
                l_s[h] = part
                a_s[h] = mixed
            else:
                factor = jnp.exp2(old - top)
                l_s[h] = l_s[h] * factor + part
                a_s[h] = a_s[h] * factor + mixed

    chunk(0, c, init=True)
    c_other(0)
    chunk(0, 1 - c)
    c_plane(4)
    for s in range(1, 5):
        if s < 4:
            gather_d.hop(s + 1)
        c_other(s)

        @pl.when(z >= s)
        def _(s=s):
            chunk(s, c)
            chunk(s, 1 - c)

    mine = pl.ds(pl.multiple_of(c * ROWS, ROWS), ROWS)
    for h in range(HEADS):
        total = jnp.sum(l_s[h], axis=1, keepdims=True)
        ctx_t[h * HD : (h + 1) * HD, mine] = jnp.transpose(a_s[h] / total).astype(BF)
    ctx_copy = sibling(3, ctx_t.at[:, mine], ctx_t.at[:, mine])
    ctx_copy.start()
    for r in range(8):
        gather_d.ready(r)
    ctx_copy.wait_recv()

    def x_copy(dx, half):
        i = (dx - 1) * 2 + half
        return rcopy(
            xs.at[dx - 1, half], xr.at[dx - 1, half], x_ss.at[i], x_sr.at[i], p.dev(dx=dx)
        )

    for dx in (2, 1, 3, 0):
        for half in (0, 1):
            zz = p.xof(dx) * 2 + half
            term = jnp.dot(
                wob[zz].reshape(320, 640), ctx_t[...], preferred_element_type=F32
            )
            if dx:
                xs[dx - 1, half] = term.astype(BF)
                x_copy(dx, half).start()
            else:
                x_own[half] = term
    for dx in (1, 3, 2):
        for half in (0, 1):
            x_copy(dx, half).wait_recv()
    for half in (0, 1):
        total = x_own[half] + (
            (xr[0, half].astype(F32) + xr[1, half].astype(F32)) + xr[2, half].astype(F32)
        )
        x_own[half] = total
    theirs = pl.ds(pl.multiple_of((1 - c) * ROWS, ROWS), ROWS)
    f_send[...] = x_own[:, :, theirs].astype(BF)
    fin_copy = sibling(4, f_send, f_recv)
    fin_copy.start()
    for half in (0, 1):
        fin[half, :, c] = x_own[half, :, mine].reshape(NY, 80, ROWS)
    fin_copy.wait_recv()
    for half in (0, 1):
        fin[half, :, 1 - c] = f_recv[half].astype(F32).reshape(NY, 80, ROWS)
    flat = fin[...].reshape(1280, ROWS)
    for i in range(10):
        out[:, i * ROWS : (i + 1) * ROWS] = jnp.transpose(
            flat[i * ROWS : (i + 1) * ROWS]
        ).astype(BF)

    gather_a.drain()
    gather_b.drain()
    gather_d.drain()
    for s in range(5):
        if s < 4:
            c_z(s).wait_send()
        for k in (1, 2, 3):
            c_y(s, k).wait_send()
        c_sib(s).wait_send()
    for cp in (hid_copy, kv_copy, q_copy, ctx_copy, fin_copy):
        cp.wait_send()
    for dx in (1, 2, 3):
        for half in (0, 1):
            x_copy(dx, half).wait_send()


def local(hidden, w_query, w_keyval, w_out, episode_lengths):
    half = np.arange(HD // 2, dtype=np.float64)
    freq = (1000000.0 ** (-(half * 2.0) / HD)).astype(np.float32)
    freq = jnp.asarray(np.concatenate([freq, freq])[None, :])
    vmem = pl.BlockSpec(memory_space=pltpu.VMEM)
    dma = pltpu.SemaphoreType.DMA
    gather_sems = [dma((7,)), dma((8,)), dma((24,)), dma((24,))]
    return pl.pallas_call(
        kernel,
        out_shape=jax.ShapeDtypeStruct((ROWS, 1280), BF),
        in_specs=[pl.BlockSpec(memory_space=pltpu.SMEM)] + [vmem] * 5,
        out_specs=vmem,
        scratch_shapes=[
            pltpu.VMEM((2, ROWS, 5120), BF),
            pltpu.VMEM((NZ, NY, 2, 80, 640), BF),
            pltpu.VMEM((NZ, NY, 2, 80, 256), BF),
            pltpu.VMEM((NZ, NY, 80, 640), BF),
            pltpu.VMEM((NZ, 2, NY, ROWS, 2 * HD), BF),
            pltpu.VMEM((2, ROWS, 256), F32),
            pltpu.VMEM((2, ROWS, 640), F32),
            pltpu.VMEM((ROWS, 256), F32),
            pltpu.VMEM((ROWS, 640), F32),
            pltpu.VMEM((HEADS, ROWS, HD), BF),
            pltpu.VMEM((ROWS, HD), jnp.int32),
            pltpu.VMEM((ROWS, HD), F32),
            pltpu.VMEM((ROWS, HD), F32),
            pltpu.VMEM((HEADS, ROWS, HD), F32),
            pltpu.VMEM((HEADS, ROWS, HD), F32),
            pltpu.VMEM((HEADS, ROWS, HD), F32),
            pltpu.VMEM((640, 2 * ROWS), BF),
            pltpu.VMEM((3, 2, 320, 2 * ROWS), BF),
            pltpu.VMEM((3, 2, 320, 2 * ROWS), BF),
            pltpu.VMEM((2, 320, 2 * ROWS), F32),
            pltpu.VMEM((2, 320, ROWS), BF),
            pltpu.VMEM((2, 320, ROWS), BF),
            pltpu.VMEM((2, NY, 2, 80, ROWS), F32),
        ]
        + gather_sems * 3
        + [dma((4,)), dma((5,)), dma((15,)), dma((15,)), dma((5,)), dma((5,))]
        + [dma((5,)), dma((5,)), dma((6,)), dma((6,))],
        name="layer",
        compiler_params=pltpu.CompilerParams(
            collective_id=0, has_side_effects=True, vmem_limit_bytes=56 * 2**20
        ),
    )(
        episode_lengths,
        hidden,
        w_query,
        w_keyval.reshape(80, 256),
        w_out.T,
        freq,
    )


def solution(mesh):
    placed = (P("ctx", None), P("ctx", "tp"), P("ctx", "tp", None), P("tp", "ctx"), P())
    return jax.shard_map(
        local, mesh=mesh, in_specs=placed, out_specs=P("ctx", "tp"), check_vma=False
    )
```

time: 606 us -> 116 us (0.19); the launches traced: 596 us -> 114 us
  waiting for transfers between devices: 325 us -> 0 us
  matrix products: 147 us -> 0 us
  Pallas kernels: 0 us -> 113 us
  other arithmetic: 54.2 us -> 0 us
  local copies, waits for them, and re-layouts: 52 us -> 1.72 us
  between operations: 13.6 us -> 0.01 us
    all_gather x5 -> x0, waiting for transfers between devices: 301 us -> none  [the longest x1 83.8 us: local(): lax.all_gather(w_keyval, 'ctx', axis=0, tiled=True)]
    dot_general x131 -> x0, matrix products: 147 us -> none  [the longest x64 69.7 us: attend_block(): jnp.einsum('hgqk,khd->hgqd', weights_exp.astype(jnp.bfloat16), value_rows...]
    pallas_call x0 -> x1, Pallas kernels: none -> 113 us  [local(): pl.pallas_call(kernel, out_shape=jax.ShapeDtypeStruct((ROWS, 1280), BF),...]
    add x129 -> x0, other arithmetic: 42.1 us -> none  [the longest x65 41.4 us: local(): tokens_at = ctx_index * tok_rows + jnp.arange(tok_rows, dtype=jnp.int32)]
    dynamic_slice x64 -> x0, local copies, waits for them, and re-layouts: 37.5 us -> none  [local(): lax.scan(scan_step, empty, (key_blocks, value_blocks, block_firsts))]
    reduce_scatter x1 -> x0, waiting for transfers between devices: 22.1 us -> none  [local(): lax.psum_scatter(terms.astype(jnp.bfloat16), 'tp', scatter_dimension=1, t...]
    unnamed x5 -> x1, local copies, waits for them, and re-layouts: 8.35 us -> 1.72 us
  transfers between devices with their start and end apart: 6 -> 0, of which waited for: 5 -> 0; matrix products, arithmetic and copies ran while one was open for 40% -> 0% of each run, Pallas kernels for 0% -> 0%
where the time goes in v1:
time: 116 us; the launch traced here: 114 us
  Pallas kernels  113 us (97%)
  local copies, waits for them, and re-layouts  1.72 us (1%)
    pallas_call x1, Pallas kernels, local(): pl.pallas_call(kernel, out_shape=jax.ShapeDtypeStruct((ROWS, 1280), BF),...  113 us

profile of v1, /device:TPU:1, one launch (start us, length us, event | category | flops | bytes accessed | tf_op | source)
XLA Modules:
  0.0 114.3 jit_solution(14948045865270326365)
XLA Ops:
  0.0 112.6 %layer.1 = bf16[128,1280]{1,0:T(8,128)(2,1)} custom-call(s32[16]{0:T(128)} %lens.1, bf16[128,5120]{1,0:T(8,128)(2,1)} %hid.1, bf16[80,640]{1,0:T(8,128)(2,1)} %wq.1, bf16[80,256]{1,0:T(8,128)(2,1)} %bitcast.3, bf16[80,640]{1,0:T(8,128)(2,1)} %bitcast.2, f32[1,128]{1,0:T(1,128)} %constant.2.clone.freq), custom_call_target="tpu_custom_call" | custom-call | tf_op jit(solution)/shard_map/layer/pallas_call | solution.py:435
  112.6 1.7 %copy.8 = bf16[128,1280]{1,0:T(8,128)(2,1)} copy(bf16[128,1280]{1,0:T(8,128)(2,1)} %layer.1) | data formatting | bytes 655360

commit v2 on v1

v2 whole, which is shorter than its diff:
```python
import math

import jax
import jax.numpy as jnp
import numpy as np
from jax import lax
from jax.experimental import pallas as pl
from jax.experimental.pallas import tpu as pltpu
from jax.sharding import PartitionSpec as P

MESH = pl.DeviceIdType.MESH
NZ, NY, NX = 8, 4, 4
ROWS = 128
HEADS = 5
HD = 128
NEG = -1e30
F32 = jnp.float32
BF = jnp.bfloat16


class Place:
    def __init__(self):
        index = lax.axis_index("ctx")
        self.index = index
        self.z = index // (2 * NY)
        self.y = lax.rem(index // 2, NY)
        self.c = lax.rem(index, 2)
        self.x = lax.axis_index("tp")

    def zof(self, dz):
        return lax.rem(self.z + (dz + NZ), NZ)

    def yof(self, dy):
        return lax.rem(self.y + (dy + NY), NY)

    def xof(self, dx):
        return lax.rem(self.x + (dx + NX), NX)

    def dev(self, dz=0, dy=0, dc=0, dx=0):
        c = 1 - self.c if dc else self.c
        return ((self.zof(dz) * NY + self.yof(dy)) * 2 + c, self.xof(dx))


def rcopy(src, dst, ssem, rsem, dev):
    return pltpu.make_async_remote_copy(
        src_ref=src, dst_ref=dst, send_sem=ssem, recv_sem=rsem, device_id=dev, device_id_type=MESH
    )


class Ring:
    def __init__(self, place, block, sems, sign):
        self.p = place
        self.block = block
        self.zs, self.zr, self.ss, self.sr = sems
        self.sign = sign

    def zslot(self, r):
        if r <= 4:
            return self.p.zof(-self.sign * r)
        return self.p.zof(self.sign * (r - 4))

    def mine(self, r):
        return self.block(self.zslot(r), self.p.c)

    def zcopy(self, hop, right):
        ref = self.mine(hop if right or not hop else hop + 4)
        i, j = (hop, hop + 1) if right else (4 + hop, 5 + hop)
        step = self.sign if right else -self.sign
        return rcopy(ref, ref, self.zs.at[i], self.zr.at[j], self.p.dev(dz=step))

    def zwait(self, r):
        ref = self.mine(r)
        rcopy(ref, ref, self.zs.at[0], self.zr.at[r], self.p.dev(dz=1)).wait_recv()

    def pair(self, r):
        ref = self.mine(r)
        return rcopy(ref, ref, self.ss.at[r], self.sr.at[r], self.p.dev(dc=1))

    def ready(self, r):
        ref = self.block(self.zslot(r), 1 - self.p.c)
        rcopy(ref, ref, self.ss.at[r], self.sr.at[r], self.p.dev(dc=1)).wait_recv()

    def start(self):
        self.zcopy(0, True).start()
        self.zcopy(0, False).start()
        self.pair(0).start()

    def hop(self, s):
        self.zwait(s)
        if s < 4:
            self.zcopy(s, True).start()
            self.zwait(4 + s)
        if s < 3:
            self.zcopy(s, False).start()
        self.pair(s).start()
        if s < 4:
            self.pair(4 + s).start()

    def drain(self):
        for hop in range(4):
            self.zcopy(hop, True).wait_send()
        for hop in range(3):
            self.zcopy(hop, False).wait_send()
        for r in range(8):
            self.pair(r).wait_send()


class Tree(Ring):
    LEGS = ((0, 2, 2), (0, -2, 6), (0, 1, 1), (0, -1, 5), (2, 2, 4), (2, 1, 3), (6, -1, 7))

    def leg(self, i):
        slot, step, to = self.LEGS[i]
        ref = self.mine(slot)
        return rcopy(ref, ref, self.zs.at[i], self.zr.at[to], self.p.dev(dz=step))

    def start(self):
        for i in range(4):
            self.leg(i).start()
        self.pair(0).start()

    def arrive(self, slots, legs=()):
        for r in slots:
            self.zwait(r)
        for i in legs:
            self.leg(i).start()
        for r in slots:
            self.pair(r).start()

    def drain(self):
        for i in range(7):
            self.leg(i).wait_send()
        for r in range(8):
            self.pair(r).wait_send()


ORDER = (1, 3, 2)


def kernel(
    lens, hid, wq, wkv, wot, freq, out,
    hx, hr, wqb, wkvb, wob, kvb, acc_kv, acc_q, ks, kr, qs, qr, qb, tok_first, cos_t, sin_t,
    m_s, l_s, a_s, ctx_t, xs, xr, x_own,
    *sems,
):
    p = Place()
    z, y, c, x = p.z, p.y, p.c, p.x
    a_sems, b_sems, d_sems = sems[0:4], sems[4:8], sems[8:12]
    c_zs, c_zr, c_ys, c_yr, c_ss, c_sr = sems[12:18]
    h_ss, h_sr, g_ss, g_sr, k_ss, k_sr, q_ss, q_sr, d_ys, d_yr, x_ss, x_sr = sems[18:30]

    barrier = pltpu.get_barrier_semaphore()
    peers = [dict(dz=d) for d in (1, -1, 2, -2)]
    peers += [dict(dy=d) for d in (1, 2, 3)] + [dict(dc=1)] + [dict(dx=d) for d in (1, 2, 3)]
    for d in peers:
        pl.semaphore_signal(barrier, inc=1, device_id=p.dev(**d), device_id_type=MESH)

    wkvb[z, c] = wkv[...]
    wqb[z, c] = wq[...]
    wob[z, c, y] = wot[...]

    lane = lax.broadcasted_iota(jnp.int32, (ROWS, HD), 1)
    for yy in range(NY):
        shift = 32 * yy
        rest = [None, None]
        for zz in range(NZ):
            at = zz * 640 + 128 * yy
            w0 = hid[:, at : at + 128]
            w1 = hid[:, at + 128 : at + 256].astype(F32)
            if yy:
                back = HD - shift
                w0 = jnp.where(
                    lane < back,
                    pltpu.roll(w0.astype(F32), back, 1),
                    pltpu.roll(w1, back, 1),
                ).astype(BF)
            hx[yy, :, zz * 128 : (zz + 1) * 128] = w0
            turn = (32 * (zz % 4) - shift) % HD
            tail = pltpu.roll(w1, turn, 1) if turn else w1
            i = zz // 4
            rest[i] = tail if zz % 4 == 0 else jnp.where(lane // 32 == zz % 4, tail, rest[i])
        for i in range(2):
            hx[yy, :, 1024 + i * 128 : 1152 + i * 128] = rest[i].astype(BF)
    hr[y] = hx[y]

    for k in (1, 2, 3):

        @pl.when(y + k < NY)
        def _(k=k):
            kvb[z, c, y + k] = jnp.zeros((ROWS, 2 * HD), BF)

        @pl.when(y - k >= 0)
        def _(k=k):
            kvb[p.zof(-4), c, y - k] = jnp.zeros((ROWS, 2 * HD), BF)

    pl.semaphore_wait(barrier, len(peers))

    ring_a = Tree(p, lambda zz, cc: wkvb.at[zz, cc], a_sems, 1)
    ring_b = Ring(p, lambda zz, cc: wqb.at[zz, cc], b_sems, -1)
    ring_d = Ring(p, lambda zz, cc: wob.at[zz, cc], d_sems, 1)

    def part(xx):
        return pl.ds(pl.multiple_of(64 + 16 * xx, 16), 16)

    def h_copy(k):
        return rcopy(
            hx.at[p.yof(k), 0:64], hr.at[y, 0:64], h_ss.at[k - 1], h_sr.at[k - 1], p.dev(dy=k)
        )

    def h_part(k):
        return rcopy(
            hx.at[p.yof(k), part(x)], hr.at[y, part(x)], h_ss.at[k + 2], h_sr.at[k + 2],
            p.dev(dy=k),
        )

    def h_part_wait(k):
        ref = hr.at[p.yof(-k), part(x)]
        rcopy(ref, ref, h_ss.at[k + 2], h_sr.at[k + 2], p.dev(dy=k)).wait_recv()

    def h_on(k, dx, back=False):
        i = (k - 1) * 3 + dx - 1
        ref = hr.at[p.yof(-k), part(p.xof(-dx) if back else x)]
        return rcopy(ref, ref, g_ss.at[i], g_sr.at[i], p.dev(dx=dx))

    def k_copy(k):
        return rcopy(
            ks.at[p.yof(k)], kr.at[k - 1], k_ss.at[k - 1], k_sr.at[k - 1], p.dev(dy=k)
        )

    def q_copy(k):
        return rcopy(
            qs.at[p.yof(k)], qr.at[k - 1], q_ss.at[k - 1], q_sr.at[k - 1], p.dev(dy=k)
        )

    def d_copy(k, dy=0):
        ref = wob.at[z, c, p.yof(dy)]
        return rcopy(ref, ref, d_ys.at[k - 1], d_yr.at[k - 1], p.dev(dy=k))

    ring_a.start()
    for k in ORDER:
        h_part(k).start()
    for k in ORDER:
        h_copy(k).start()
    ring_b.start()

    tok = p.index * ROWS + lax.broadcasted_iota(jnp.int32, (ROWS, HD), 0)
    first = jnp.zeros((ROWS, HD), jnp.int32)
    end = jnp.int32(0)
    for i in range(16):
        end = end + lens[i]
        first = jnp.maximum(first, jnp.where(end <= tok, end, 0))
    tok_first[...] = first
    angle = (tok - first).astype(F32) * freq[...]
    cos_t[...] = jnp.cos(angle)
    sine = jnp.sin(angle)
    sin_t[...] = jnp.where(lane < HD // 2, -sine, sine)

    def rotate(v):
        return v * cos_t[...] + pltpu.roll(v, HD // 2, 1) * sin_t[...]

    def project(ring, buf, acc, send, r, width):
        if r < 8:
            ring.ready(r)
            zz = ring.zslot(r)
            left = hr[:, :, pl.ds(pl.multiple_of(zz * HD, HD), HD)].reshape(NY * ROWS, HD)
            right = buf[zz].reshape(160, width)[:HD]
        else:
            left = hr[:, :, 1024:1280].reshape(NY * ROWS, 256)
            right = buf[...].reshape(NZ, 160, width)[:, HD:].reshape(256, width)
        term = jnp.dot(left, right, preferred_element_type=F32).reshape(NY, ROWS, width)
        if r == 0:
            acc[...] = term
        elif r < 8:
            acc[...] += term
        else:
            term = acc[...] + term
            acc[...] = term
            send[...] = term.astype(BF)

    def c_block(s, dy=0):
        return kvb.at[p.zof(-s), c, p.yof(dy)]

    c_legs = ((0, 2, 2), (0, 1, 1), (0, -2, -2), (2, 1, 3), (-2, -2, 4))

    def c_z(i):
        plane, step, to = c_legs[i]
        return rcopy(
            c_block(plane), c_block(plane), c_zs.at[i], c_zr.at[max(to, 0)],
            p.dev(dz=step),
        )

    def c_zwait(s):
        ref = c_block(s)
        rcopy(ref, ref, c_zs.at[0], c_zr.at[max(s, 0)], p.dev(dz=1)).wait_recv()

    def c_y(s, k):
        i = s * 3 + k - 1
        return rcopy(c_block(s), c_block(s), c_ys.at[i], c_yr.at[i], p.dev(dy=k))

    def c_when(s, k, sending, act):
        if s == 0:
            pl.when(y + k < NY if sending else y - k >= 0)(act)
        elif s == 4:
            pl.when(y + k >= NY if sending else y - k < 0)(act)
        else:
            act()

    def c_sib(s):
        ref = kvb.at[p.zof(-s), c]
        return rcopy(ref, ref, c_ss.at[s], c_sr.at[s], p.dev(dc=1))

    def c_hop(s):
        if s:
            c_zwait(s)
        for i, leg in enumerate(c_legs):
            if leg[0] == s:
                c_z(i).start()
        if s < 0:
            return
        for k in ORDER:
            c_when(s, k, True, lambda: c_y(s, k).start())

    def c_plane(s):
        for k in ORDER:
            i = s * 3 + k - 1
            ref = c_block(s, -k)
            c_when(
                s, k, False,
                lambda: rcopy(ref, ref, c_ys.at[i], c_yr.at[i], p.dev(dy=k)).wait_recv(),
            )
        c_sib(s).start()

    def c_other(s):
        ref = kvb.at[p.zof(-s), 1 - c]
        rcopy(ref, ref, c_ss.at[s], c_sr.at[s], p.dev(dc=1)).wait_recv()

    ring_a.arrive((2, 6), (4, 5, 6))
    for k in ORDER:
        h_part_wait(k)
        for dx in ORDER:
            h_on(k, dx).start()
    ring_a.arrive((1, 5))
    ring_b.hop(1)
    ring_a.arrive((3, 4, 7))
    for k in ORDER:
        d_copy(k).start()
    ring_b.hop(2)
    for k in ORDER:
        h_copy(k).wait_recv()
        for dx in ORDER:
            h_on(k, dx, True).wait_recv()
    for r in (0, 1, 5, 2, 6, 3, 7, 4, 8):
        project(ring_a, wkvb, acc_kv, ks, r, 256)
    for k in ORDER:
        k_copy(k).start()
    ring_b.hop(3)
    for k in ORDER:
        d_copy(k, -k).wait_recv()
    ring_d.start()
    for k in ORDER:
        k_copy(k).wait_recv()
    keyval = (acc_kv[y] + kr[0].astype(F32)) + (kr[1].astype(F32) + kr[2].astype(F32))
    kvb[z, c, y] = jnp.concatenate(
        [rotate(keyval[:, :HD]).astype(BF), keyval[:, HD:].astype(BF)], axis=1
    )
    c_hop(0)
    ring_b.hop(4)
    for r in (0, 1, 5, 2, 6, 3, 7, 4, 8):
        project(ring_b, wqb, acc_q, qs, r, 640)
    for k in ORDER:
        q_copy(k).start()
    c_hop(2)
    c_hop(-2)
    c_hop(1)
    c_hop(3)
    c_hop(4)
    c_plane(0)
    c_plane(1)
    for k in ORDER:
        q_copy(k).wait_recv()
    query = (acc_q[y] + qr[0].astype(F32)) + (qr[1].astype(F32) + qr[2].astype(F32))
    for h in range(HEADS):
        qb[h] = rotate(query[:, h * HD : (h + 1) * HD]).astype(BF)
    ring_d.hop(1)
    c_plane(2)

    scale = math.log2(math.e) / math.sqrt(HD)
    spot = lax.broadcasted_iota(jnp.int32, (ROWS, 4 * HD), 1)
    spot = (spot // ROWS) * (2 * ROWS) + lax.rem(spot, ROWS)
    wide_tok = p.index * ROWS + lax.broadcasted_iota(jnp.int32, (ROWS, 4 * HD), 0)

    def chunk(s, core, init=False):
        zp = p.zof(-s)
        key_at = spot + (zp * (2 * NY * ROWS) + core * ROWS)
        wide_first = jnp.concatenate([tok_first[...]] * 4, axis=1)
        bias = jnp.where((key_at >= wide_first) & (key_at <= wide_tok), 0.0, NEG)
        keys = kvb[zp, core, :, :, 0:HD].reshape(4 * ROWS, HD)
        values = kvb[zp, core, :, :, HD : 2 * HD].reshape(4 * ROWS, HD)
        for h in range(HEADS):
            score = lax.dot_general(
                qb[h], keys, (((1,), (1,)), ((), ())), preferred_element_type=F32
            )
            score = score * scale + bias
            top = jnp.broadcast_to(jnp.max(score, axis=1, keepdims=True), (ROWS, HD))
            if not init:
                old = m_s[h]
                top = jnp.maximum(old, top)
            weight = jnp.exp2(score - jnp.concatenate([top] * 4, axis=1))
            part = (weight[:, :HD] + weight[:, HD : 2 * HD]) + (
                weight[:, 2 * HD : 3 * HD] + weight[:, 3 * HD :]
            )
            mixed = jnp.dot(weight.astype(BF), values, preferred_element_type=F32)
            m_s[h] = top
            if init:
                l_s[h] = part
                a_s[h] = mixed
            else:
                factor = jnp.exp2(old - top)
                l_s[h] = l_s[h] * factor + part
                a_s[h] = a_s[h] * factor + mixed

    chunk(0, c, init=True)
    c_other(0)
    chunk(0, 1 - c)
    c_plane(3)
    c_plane(4)
    for s in range(1, 5):
        c_other(s)

        @pl.when(z >= s)
        def _(s=s):
            chunk(s, c)
            chunk(s, 1 - c)

        if s == 2:
            ring_d.hop(2)

    for h in range(HEADS):
        total = jnp.sum(l_s[h], axis=1, keepdims=True)
        ctx_t[h * HD : (h + 1) * HD, :] = jnp.transpose(a_s[h] / total).astype(BF)

    def x_copy(dx, half):
        i = (dx - 1) * 2 + half
        return rcopy(
            xs.at[dx - 1, half], xr.at[dx - 1, half], x_ss.at[i], x_sr.at[i], p.dev(dx=dx)
        )

    for r in (0, 1, 5, 2, 6, 3, 7, 4):
        if r == 2:
            ring_d.hop(3)
        elif r == 3:
            ring_d.hop(4)
        ring_d.ready(r)
        zz = ring_d.zslot(r)
        half = lax.rem(zz, 2)
        dx = lax.rem(zz // 2 - x + NX, NX)
        term = jnp.dot(wob[zz].reshape(640, 640), ctx_t[...], preferred_element_type=F32)
        term = term.reshape(2, NY, 80, ROWS)

        @pl.when(dx == 0)
        def _(term=term, half=half):
            for core in (0, 1):
                x_own[half, :, core] = term[core]

        @pl.when(dx > 0)
        def _(term=term, half=half, dx=dx):
            for core in (0, 1):
                xs[dx - 1, half, :, core] = term[core].astype(BF)
            x_copy(dx, half).start()

    for half in (0, 1):
        for dx in ORDER:
            x_copy(dx, half).wait_recv()
        total = x_own[half] + (
            (xr[0, half].astype(F32) + xr[1, half].astype(F32)) + xr[2, half].astype(F32)
        )
        flat = total.reshape(640, ROWS)
        for i in range(5):
            out[:, half * 640 + i * ROWS : half * 640 + (i + 1) * ROWS] = jnp.transpose(
                flat[i * ROWS : (i + 1) * ROWS]
            ).astype(BF)

    ring_a.drain()
    ring_b.drain()
    ring_d.drain()
    for s in range(5):
        c_z(s).wait_send()
        for k in ORDER:
            c_when(s, k, True, lambda: c_y(s, k).wait_send())
        c_sib(s).wait_send()
    for k in ORDER:
        h_copy(k).wait_send()
        h_part(k).wait_send()
        for dx in ORDER:
            h_on(k, dx).wait_send()
        k_copy(k).wait_send()
        q_copy(k).wait_send()
        d_copy(k).wait_send()
        for half in (0, 1):
            x_copy(k, half).wait_send()


def local(hidden, w_query, w_keyval, w_out, episode_lengths):
    half = np.arange(HD // 2, dtype=np.float64)
    freq = (1000000.0 ** (-(half * 2.0) / HD)).astype(np.float32)
    freq = jnp.asarray(np.concatenate([freq, freq])[None, :])
    vmem = pl.BlockSpec(memory_space=pltpu.VMEM)
    dma = pltpu.SemaphoreType.DMA
    return pl.pallas_call(
        kernel,
        out_shape=jax.ShapeDtypeStruct((ROWS, 1280), BF),
        in_specs=[pl.BlockSpec(memory_space=pltpu.SMEM)] + [vmem] * 5,
        out_specs=vmem,
        scratch_shapes=[
            pltpu.VMEM((NY, ROWS, 1280), BF),
            pltpu.VMEM((NY, ROWS, 1280), BF),
            pltpu.VMEM((NZ, 2, 80, 640), BF),
            pltpu.VMEM((NZ, 2, 80, 256), BF),
            pltpu.VMEM((NZ, 2, NY, 80, 640), BF),
            pltpu.VMEM((NZ, 2, NY, ROWS, 2 * HD), BF),
            pltpu.VMEM((NY, ROWS, 256), F32),
            pltpu.VMEM((NY, ROWS, 640), F32),
            pltpu.VMEM((NY, ROWS, 256), BF),
            pltpu.VMEM((3, ROWS, 256), BF),
            pltpu.VMEM((NY, ROWS, 640), BF),
            pltpu.VMEM((3, ROWS, 640), BF),
            pltpu.VMEM((HEADS, ROWS, HD), BF),
            pltpu.VMEM((ROWS, HD), jnp.int32),
            pltpu.VMEM((ROWS, HD), F32),
            pltpu.VMEM((ROWS, HD), F32),
            pltpu.VMEM((HEADS, ROWS, HD), F32),
            pltpu.VMEM((HEADS, ROWS, HD), F32),
            pltpu.VMEM((HEADS, ROWS, HD), F32),
            pltpu.VMEM((640, ROWS), BF),
            pltpu.VMEM((3, 2, NY, 2, 80, ROWS), BF),
            pltpu.VMEM((3, 2, NY, 2, 80, ROWS), BF),
            pltpu.VMEM((2, NY, 2, 80, ROWS), F32),
        ]
        + [dma((7,)), dma((8,)), dma((8,)), dma((8,))] * 3
        + [dma((5,)), dma((5,)), dma((15,)), dma((15,)), dma((5,)), dma((5,))]
        + [dma((6,)), dma((6,)), dma((9,)), dma((9,))]
        + [dma((3,))] * 6
        + [dma((6,)), dma((6,))],
        name="layer",
        compiler_params=pltpu.CompilerParams(
            collective_id=0, has_side_effects=True, vmem_limit_bytes=56 * 2**20
        ),
    )(
        episode_lengths,
        hidden,
        w_query,
        w_keyval.reshape(80, 256),
        w_out.T,
        freq,
    )


def solution(mesh):
    placed = (P("ctx", None), P("ctx", "tp"), P("ctx", "tp", None), P("tp", "ctx"), P())
    return jax.shard_map(
        local, mesh=mesh, in_specs=placed, out_specs=P("ctx", "tp"), check_vma=False
    )
```

time: 116 us -> 93.9 us (0.81)
  the two profiles are of different devices: /device:TPU:1 before, /device:TPU:4 now
where the time goes in v2:
time: 93.9 us; the launch traced here: 93.8 us
  Pallas kernels  92 us (98%)
  local copies, waits for them, and re-layouts  1.72 us (2%)
    pallas_call x1, Pallas kernels, local(): pl.pallas_call(kernel, out_shape=jax.ShapeDtypeStruct((ROWS, 1280), BF),...  92 us

profile of v2, /device:TPU:4, one launch (start us, length us, event | category | flops | bytes accessed | tf_op | source)
XLA Modules:
  0.0 93.8 jit_solution(3173295813530900211)
XLA Ops:
  0.0 92.0 %layer.1 = bf16[128,1280]{1,0:T(8,128)(2,1)} custom-call(s32[16]{0:T(128)} %lens.1, bf16[128,5120]{1,0:T(8,128)(2,1)} %hid.1, bf16[80,640]{1,0:T(8,128)(2,1)} %wq.1, bf16[80,256]{1,0:T(8,128)(2,1)} %bitcast.3, bf16[80,640]{1,0:T(8,128)(2,1)} %bitcast.2, f32[1,128]{1,0:T(1,128)} %constant.2.clone.freq), custom_call_target="tpu_custom_call" | custom-call | tf_op jit(solution)/shard_map/layer/pallas_call | solution.py:508
  92.1 1.7 %copy.8 = bf16[128,1280]{1,0:T(8,128)(2,1)} copy(bf16[128,1280]{1,0:T(8,128)(2,1)} %layer.1) | data formatting | bytes 655360

commit v3 on v2

--- a/solution.py
+++ b/solution.py
@@ -138,15 +138,15 @@
 
 def kernel(
     lens, hid, wq, wkv, wot, freq, out,
-    hx, hr, wqb, wkvb, wob, kvb, acc_kv, acc_q, ks, kr, qs, qr, qb, tok_first, cos_t, sin_t,
-    m_s, l_s, a_s, ctx_t, xs, xr, x_own,
+    hx, hr, wqb, wqc, wkvb, wob, kvb, acc_kv, acc_q, acc_r, ks, kr, qs, qr, rs, rr, qb, tok_first, cos_t, sin_t,
+    m_s, l_s, a_s, ctx, xs, xr, x_own, f_send, f_recv, fin,
     *sems,
 ):
     p = Place()
     z, y, c, x = p.z, p.y, p.c, p.x
-    a_sems, b_sems, d_sems = sems[0:4], sems[4:8], sems[8:12]
-    c_zs, c_zr, c_ys, c_yr, c_ss, c_sr = sems[12:18]
-    h_ss, h_sr, g_ss, g_sr, k_ss, k_sr, q_ss, q_sr, d_ys, d_yr, x_ss, x_sr = sems[18:30]
+    a_sems, b_sems, e_sems, d_sems = sems[0:4], sems[4:8], sems[8:12], sems[12:16]
+    c_zs, c_zr, c_ys, c_yr, c_ss, c_sr = sems[16:22]
+    h_ss, h_sr, g_ss, g_sr, k_ss, k_sr, q_ss, q_sr, r_ss, r_sr, t_ss, t_sr, f_ss, f_sr, x_ss, x_sr = sems[22:38]
 
     barrier = pltpu.get_barrier_semaphore()
     peers = [dict(dz=d) for d in (1, -1, 2, -2)]
@@ -155,8 +155,9 @@
         pl.semaphore_signal(barrier, inc=1, device_id=p.dev(**d), device_id_type=MESH)
 
     wkvb[z, c] = wkv[...]
-    wqb[z, c] = wq[...]
-    wob[z, c, y] = wot[...]
+    wqb[z, c] = wq[:, :256]
+    wqc[z, c] = wq[:, 256:]
+    wob[z, c] = wot[...]
 
     lane = lax.broadcasted_iota(jnp.int32, (ROWS, HD), 1)
     for yy in range(NY):
@@ -186,17 +187,18 @@
 
         @pl.when(y + k < NY)
         def _(k=k):
-            kvb[z, c, y + k] = jnp.zeros((ROWS, 2 * HD), BF)
+            kvb[z, c, y + k] = jnp.zeros((2, ROWS, HD), BF)
 
         @pl.when(y - k >= 0)
         def _(k=k):
-            kvb[p.zof(-4), c, y - k] = jnp.zeros((ROWS, 2 * HD), BF)
+            kvb[p.zof(-4), c, y - k] = jnp.zeros((2, ROWS, HD), BF)
 
     pl.semaphore_wait(barrier, len(peers))
 
     ring_a = Tree(p, lambda zz, cc: wkvb.at[zz, cc], a_sems, 1)
     ring_b = Ring(p, lambda zz, cc: wqb.at[zz, cc], b_sems, -1)
-    ring_d = Ring(p, lambda zz, cc: wob.at[zz, cc], d_sems, 1)
+    ring_e = Ring(p, lambda zz, cc: wqc.at[zz, cc], e_sems, 1)
+    ring_d = Ring(p, lambda zz, cc: wob.at[zz, cc], d_sems, -1)
 
     def part(xx):
         return pl.ds(pl.multiple_of(64 + 16 * xx, 16), 16)
@@ -231,9 +233,10 @@
             qs.at[p.yof(k)], qr.at[k - 1], q_ss.at[k - 1], q_sr.at[k - 1], p.dev(dy=k)
         )
 
-    def d_copy(k, dy=0):
-        ref = wob.at[z, c, p.yof(dy)]
-        return rcopy(ref, ref, d_ys.at[k - 1], d_yr.at[k - 1], p.dev(dy=k))
+    def r_copy(k):
+        return rcopy(
+            rs.at[p.yof(k)], rr.at[k - 1], r_ss.at[k - 1], r_sr.at[k - 1], p.dev(dy=k)
+        )
 
     ring_a.start()
     for k in ORDER:
@@ -248,7 +251,13 @@
     for i in range(16):
         end = end + lens[i]
         first = jnp.maximum(first, jnp.where(end <= tok, end, 0))
-    tok_first[...] = first
+    row_tok = p.index * ROWS + lax.broadcasted_iota(jnp.int32, (1, ROWS), 1)
+    row_first = jnp.zeros((1, ROWS), jnp.int32)
+    end = jnp.int32(0)
+    for i in range(16):
+        end = end + lens[i]
+        row_first = jnp.maximum(row_first, jnp.where(end <= row_tok, end, 0))
+    tok_first[...] = row_first
     angle = (tok - first).astype(F32) * freq[...]
     cos_t[...] = jnp.cos(angle)
     sine = jnp.sin(angle)
@@ -340,9 +349,8 @@
             h_on(k, dx).start()
     ring_a.arrive((1, 5))
     ring_b.hop(1)
+    ring_e.start()
     ring_a.arrive((3, 4, 7))
-    for k in ORDER:
-        d_copy(k).start()
     ring_b.hop(2)
     for k in ORDER:
         h_copy(k).wait_recv()
@@ -352,135 +360,186 @@
         project(ring_a, wkvb, acc_kv, ks, r, 256)
     for k in ORDER:
         k_copy(k).start()
+    ring_e.hop(1)
     ring_b.hop(3)
-    for k in ORDER:
-        d_copy(k, -k).wait_recv()
-    ring_d.start()
+    for r in (0, 1, 5, 2, 6):
+        project(ring_b, wqb, acc_q, qs, r, 256)
+    ring_e.hop(2)
+    ring_b.hop(4)
+    for r in (3, 7, 4, 8):
+        project(ring_b, wqb, acc_q, qs, r, 256)
+    for k in ORDER:
+        q_copy(k).start()
+    ring_e.hop(3)
     for k in ORDER:
         k_copy(k).wait_recv()
     keyval = (acc_kv[y] + kr[0].astype(F32)) + (kr[1].astype(F32) + kr[2].astype(F32))
-    kvb[z, c, y] = jnp.concatenate(
-        [rotate(keyval[:, :HD]).astype(BF), keyval[:, HD:].astype(BF)], axis=1
-    )
+    kvb[z, c, y, 0] = rotate(keyval[:, :HD]).astype(BF)
+    kvb[z, c, y, 1] = jnp.transpose(keyval[:, HD:]).astype(BF)
     c_hop(0)
-    ring_b.hop(4)
-    for r in (0, 1, 5, 2, 6, 3, 7, 4, 8):
-        project(ring_b, wqb, acc_q, qs, r, 640)
-    for k in ORDER:
-        q_copy(k).start()
+    for r in (0, 1, 5, 2, 6):
+        project(ring_e, wqc, acc_r, rs, r, 384)
+
+    def queries(acc, got, copies, head, count):
+        for k in ORDER:
+            copies(k).wait_recv()
+        query = (acc[y] + got[0].astype(F32)) + (got[1].astype(F32) + got[2].astype(F32))
+        for h in range(count):
+            qb[:, (head + h) * HD : (head + h + 1) * HD] = jnp.transpose(
+                rotate(query[:, h * HD : (h + 1) * HD])
+            ).astype(BF)
+
+    queries(acc_q, qr, q_copy, 0, 2)
+
+    scale = math.log2(math.e) / math.sqrt(HD)
+    spot = lax.broadcasted_iota(jnp.int32, (NY * ROWS, ROWS), 0)
+    spot = (spot // ROWS) * (2 * ROWS) + lax.rem(spot, ROWS)
+
+    parts = (slice(0, 2 * ROWS), slice(2 * ROWS, HEADS * ROWS))
+
+    def chunk(s, core, part, init=False):
+        at = parts[part]
+        zp = p.zof(-s)
+        key_at = spot + (zp * (2 * NY * ROWS) + core * ROWS)
+        bias = jnp.where((key_at >= tok_first[...]) & (key_at <= row_tok), 0.0, NEG)
+        keys = kvb[zp, core, :, 0].reshape(NY * ROWS, HD)
+        values = jnp.concatenate([kvb[zp, core, i, 1] for i in range(NY)], axis=1)
+        score = jnp.dot(keys, qb[:, at], preferred_element_type=F32)
+        score = score * scale + jnp.concatenate([bias] * (2 + part), axis=1)
+        top = jnp.max(score, axis=0, keepdims=True)
+        if not init:
+            old = m_s[:, at]
+            top = jnp.maximum(old, top)
+        weight = jnp.exp2(score - top)
+        share = jnp.sum(weight, axis=0, keepdims=True)
+        mixed = jnp.dot(values, weight.astype(BF), preferred_element_type=F32)
+        m_s[:, at] = top
+        if init:
+            l_s[:, at] = share
+            a_s[:, at] = mixed
+        else:
+            factor = jnp.exp2(old - top)
+            l_s[:, at] = l_s[:, at] * factor + share
+            a_s[:, at] = a_s[:, at] * factor + mixed
+
+    def reach(s, core, which=(0, 1)):
+        @pl.when(z >= s)
+        def _():
+            for part in which:
+                chunk(s, core, part)
+
     c_hop(2)
     c_hop(-2)
+    ring_e.hop(4)
+    for r in (3, 7, 4, 8):
+        project(ring_e, wqc, acc_r, rs, r, 384)
+    for k in ORDER:
+        r_copy(k).start()
     c_hop(1)
+    ring_d.start()
+    c_plane(0)
+    chunk(0, c, 0, init=True)
+    ring_d.hop(1)
     c_hop(3)
     c_hop(4)
-    c_plane(0)
+    c_other(0)
+    chunk(0, 1 - c, 0)
     c_plane(1)
-    for k in ORDER:
-        q_copy(k).wait_recv()
-    query = (acc_q[y] + qr[0].astype(F32)) + (qr[1].astype(F32) + qr[2].astype(F32))
-    for h in range(HEADS):
-        qb[h] = rotate(query[:, h * HD : (h + 1) * HD]).astype(BF)
-    ring_d.hop(1)
     c_plane(2)
-
-    scale = math.log2(math.e) / math.sqrt(HD)
-    spot = lax.broadcasted_iota(jnp.int32, (ROWS, 4 * HD), 1)
-    spot = (spot // ROWS) * (2 * ROWS) + lax.rem(spot, ROWS)
-    wide_tok = p.index * ROWS + lax.broadcasted_iota(jnp.int32, (ROWS, 4 * HD), 0)
-
-    def chunk(s, core, init=False):
-        zp = p.zof(-s)
-        key_at = spot + (zp * (2 * NY * ROWS) + core * ROWS)
-        wide_first = jnp.concatenate([tok_first[...]] * 4, axis=1)
-        bias = jnp.where((key_at >= wide_first) & (key_at <= wide_tok), 0.0, NEG)
-        keys = kvb[zp, core, :, :, 0:HD].reshape(4 * ROWS, HD)
-        values = kvb[zp, core, :, :, HD : 2 * HD].reshape(4 * ROWS, HD)
-        for h in range(HEADS):
-            score = lax.dot_general(
-                qb[h], keys, (((1,), (1,)), ((), ())), preferred_element_type=F32
-            )
-            score = score * scale + bias
-            top = jnp.broadcast_to(jnp.max(score, axis=1, keepdims=True), (ROWS, HD))
-            if not init:
-                old = m_s[h]
-                top = jnp.maximum(old, top)
-            weight = jnp.exp2(score - jnp.concatenate([top] * 4, axis=1))
-            part = (weight[:, :HD] + weight[:, HD : 2 * HD]) + (
-                weight[:, 2 * HD : 3 * HD] + weight[:, 3 * HD :]
-            )
-            mixed = jnp.dot(weight.astype(BF), values, preferred_element_type=F32)
-            m_s[h] = top
-            if init:
-                l_s[h] = part
-                a_s[h] = mixed
-            else:
-                factor = jnp.exp2(old - top)
-                l_s[h] = l_s[h] * factor + part
-                a_s[h] = a_s[h] * factor + mixed
-
-    chunk(0, c, init=True)
-    c_other(0)
-    chunk(0, 1 - c)
+    reach(1, c, (0,))
+    queries(acc_r, rr, r_copy, 2, 3)
+    chunk(0, c, 1, init=True)
+    chunk(0, 1 - c, 1)
+    ring_d.hop(2)
+    reach(1, c, (1,))
+    c_other(1)
+    reach(1, 1 - c)
     c_plane(3)
     c_plane(4)
-    for s in range(1, 5):
-        c_other(s)
-
-        @pl.when(z >= s)
-        def _(s=s):
-            chunk(s, c)
-            chunk(s, 1 - c)
-
-        if s == 2:
-            ring_d.hop(2)
+    reach(2, c)
+    c_other(2)
+    reach(2, 1 - c)
+    ring_d.hop(3)
+    reach(3, c)
+    reach(4, c)
+    c_other(3)
+    reach(3, 1 - c)
+    ring_d.hop(4)
+    c_other(4)
+    reach(4, 1 - c)
 
     for h in range(HEADS):
-        total = jnp.sum(l_s[h], axis=1, keepdims=True)
-        ctx_t[h * HD : (h + 1) * HD, :] = jnp.transpose(a_s[h] / total).astype(BF)
-
-    def x_copy(dx, half):
-        i = (dx - 1) * 2 + half
-        return rcopy(
-            xs.at[dx - 1, half], xr.at[dx - 1, half], x_ss.at[i], x_sr.at[i], p.dev(dx=dx)
-        )
-
-    for r in (0, 1, 5, 2, 6, 3, 7, 4):
-        if r == 2:
-            ring_d.hop(3)
-        elif r == 3:
-            ring_d.hop(4)
+        at = slice(h * HD, (h + 1) * HD)
+        ctx[y, at, :] = (a_s[:, at] / l_s[:, at]).astype(BF)
+
+    def t_copy(k, dy=0):
+        ref = ctx.at[p.yof(dy)]
+        return rcopy(ref, ref, t_ss.at[k - 1], t_sr.at[k - 1], p.dev(dy=k))
+
+    t_copy(1).start()
+    t_copy(3).start()
+    for r in range(8):
         ring_d.ready(r)
-        zz = ring_d.zslot(r)
-        half = lax.rem(zz, 2)
-        dx = lax.rem(zz // 2 - x + NX, NX)
-        term = jnp.dot(wob[zz].reshape(640, 640), ctx_t[...], preferred_element_type=F32)
-        term = term.reshape(2, NY, 80, ROWS)
-
-        @pl.when(dx == 0)
-        def _(term=term, half=half):
-            for core in (0, 1):
-                x_own[half, :, core] = term[core]
-
-        @pl.when(dx > 0)
-        def _(term=term, half=half, dx=dx):
-            for core in (0, 1):
-                xs[dx - 1, half, :, core] = term[core].astype(BF)
-            x_copy(dx, half).start()
-
-    for half in (0, 1):
+
+    def x_copy(g, dx):
+        i = g * 3 + dx - 1
+        return rcopy(
+            xs.at[g, dx - 1], xr.at[g, dx - 1], x_ss.at[i], x_sr.at[i], p.dev(dx=dx)
+        )
+
+    def f_copy(g):
+        return rcopy(
+            f_send.at[g - 1], f_recv.at[g - 1], f_ss.at[g - 1], f_sr.at[g - 1], p.dev(dy=-g)
+        )
+
+    def settle(dy, part):
+        part = part.reshape(2, 2, 80, ROWS)
+        for half in (0, 1):
+            fin[half, p.yof(dy)] = part[half]
+
+    def terms(g):
+        if g:
+            t_copy(g, -g).wait_recv()
+        for dx in (2, 1, 3, 0):
+            right = ctx[p.yof(-g)]
+            left = wob[pl.ds(2 * p.xof(dx), 2)].reshape(320, 640)
+            term = jnp.dot(left, right, preferred_element_type=F32)
+            if dx:
+                xs[g, dx - 1] = term.astype(BF)
+                x_copy(g, dx).start()
+            else:
+                x_own[g] = term
+
+    def total(g):
         for dx in ORDER:
-            x_copy(dx, half).wait_recv()
-        total = x_own[half] + (
-            (xr[0, half].astype(F32) + xr[1, half].astype(F32)) + xr[2, half].astype(F32)
-        )
-        flat = total.reshape(640, ROWS)
-        for i in range(5):
-            out[:, half * 640 + i * ROWS : half * 640 + (i + 1) * ROWS] = jnp.transpose(
-                flat[i * ROWS : (i + 1) * ROWS]
-            ).astype(BF)
+            x_copy(g, dx).wait_recv()
+        part = x_own[g] + (
+            (xr[g, 0].astype(F32) + xr[g, 1].astype(F32)) + xr[g, 2].astype(F32)
+        )
+        if g:
+            f_send[g - 1] = part.astype(BF)
+            f_copy(g).start()
+        else:
+            settle(0, part)
+
+    terms(0)
+    t_copy(2).start()
+    for g in (1, 3, 2):
+        terms(g)
+    for g in (0, 1, 3, 2):
+        total(g)
+    for g in (1, 3, 2):
+        f_copy(g).wait_recv()
+        settle(g, f_recv[g - 1].astype(F32))
+    flat = fin[...].reshape(1280, ROWS)
+    for i in range(10):
+        out[:, i * ROWS : (i + 1) * ROWS] = jnp.transpose(
+            flat[i * ROWS : (i + 1) * ROWS]
+        ).astype(BF)
 
     ring_a.drain()
     ring_b.drain()
+    ring_e.drain()
     ring_d.drain()
     for s in range(5):
         c_z(s).wait_send()
@@ -494,9 +553,11 @@
             h_on(k, dx).wait_send()
         k_copy(k).wait_send()
         q_copy(k).wait_send()
-        d_copy(k).wait_send()
-        for half in (0, 1):
-            x_copy(k, half).wait_send()
+        r_copy(k).wait_send()
+        t_copy(k).wait_send()
+        f_copy(k).wait_send()
+        for g in range(NY):
+            x_copy(g, k).wait_send()
 
 
 def local(hidden, w_query, w_keyval, w_out, episode_lengths):
@@ -513,33 +574,40 @@
         scratch_shapes=[
             pltpu.VMEM((NY, ROWS, 1280), BF),
             pltpu.VMEM((NY, ROWS, 1280), BF),
+            pltpu.VMEM((NZ, 2, 80, 256), BF),
+            pltpu.VMEM((NZ, 2, 80, 384), BF),
+            pltpu.VMEM((NZ, 2, 80, 256), BF),
             pltpu.VMEM((NZ, 2, 80, 640), BF),
-            pltpu.VMEM((NZ, 2, 80, 256), BF),
-            pltpu.VMEM((NZ, 2, NY, 80, 640), BF),
-            pltpu.VMEM((NZ, 2, NY, ROWS, 2 * HD), BF),
+            pltpu.VMEM((NZ, 2, NY, 2, ROWS, HD), BF),
             pltpu.VMEM((NY, ROWS, 256), F32),
-            pltpu.VMEM((NY, ROWS, 640), F32),
+            pltpu.VMEM((NY, ROWS, 256), F32),
+            pltpu.VMEM((NY, ROWS, 384), F32),
             pltpu.VMEM((NY, ROWS, 256), BF),
             pltpu.VMEM((3, ROWS, 256), BF),
-            pltpu.VMEM((NY, ROWS, 640), BF),
-            pltpu.VMEM((3, ROWS, 640), BF),
-            pltpu.VMEM((HEADS, ROWS, HD), BF),
-            pltpu.VMEM((ROWS, HD), jnp.int32),
+            pltpu.VMEM((NY, ROWS, 256), BF),
+            pltpu.VMEM((3, ROWS, 256), BF),
+            pltpu.VMEM((NY, ROWS, 384), BF),
+            pltpu.VMEM((3, ROWS, 384), BF),
+            pltpu.VMEM((HD, HEADS * ROWS), BF),
+            pltpu.VMEM((1, ROWS), jnp.int32),
             pltpu.VMEM((ROWS, HD), F32),
             pltpu.VMEM((ROWS, HD), F32),
-            pltpu.VMEM((HEADS, ROWS, HD), F32),
-            pltpu.VMEM((HEADS, ROWS, HD), F32),
-            pltpu.VMEM((HEADS, ROWS, HD), F32),
-            pltpu.VMEM((640, ROWS), BF),
-            pltpu.VMEM((3, 2, NY, 2, 80, ROWS), BF),
-            pltpu.VMEM((3, 2, NY, 2, 80, ROWS), BF),
+            pltpu.VMEM((1, HEADS * ROWS), F32),
+            pltpu.VMEM((1, HEADS * ROWS), F32),
+            pltpu.VMEM((HD, HEADS * ROWS), F32),
+            pltpu.VMEM((NY, 640, ROWS), BF),
+            pltpu.VMEM((NY, 3, 320, ROWS), BF),
+            pltpu.VMEM((NY, 3, 320, ROWS), BF),
+            pltpu.VMEM((NY, 320, ROWS), F32),
+            pltpu.VMEM((3, 320, ROWS), BF),
+            pltpu.VMEM((3, 320, ROWS), BF),
             pltpu.VMEM((2, NY, 2, 80, ROWS), F32),
         ]
-        + [dma((7,)), dma((8,)), dma((8,)), dma((8,))] * 3
+        + [dma((7,)), dma((8,)), dma((8,)), dma((8,))] * 4
         + [dma((5,)), dma((5,)), dma((15,)), dma((15,)), dma((5,)), dma((5,))]
         + [dma((6,)), dma((6,)), dma((9,)), dma((9,))]
-        + [dma((3,))] * 6
-        + [dma((6,)), dma((6,))],
+        + [dma((3,))] * 10
+        + [dma((12,)), dma((12,))],
         name="layer",
         compiler_params=pltpu.CompilerParams(
             collective_id=0, has_side_effects=True, vmem_limit_bytes=56 * 2**20

time: 93.9 us -> 83.7 us (0.89)
  the two profiles are of different devices: /device:TPU:4 before, /device:TPU:1 now
where the time goes in v3:
time: 83.7 us; the launch traced here: 83.6 us
  Pallas kernels  81.9 us (98%)
  local copies, waits for them, and re-layouts  1.72 us (2%)
    pallas_call x1, Pallas kernels, local(): pl.pallas_call(kernel, out_shape=jax.ShapeDtypeStruct((ROWS, 1280), BF),...  81.9 us
    unnamed x1, local copies, waits for them, and re-layouts  1.72 us

profile of v3, /device:TPU:1, one launch (start us, length us, event | category | flops | bytes accessed | tf_op | source)
XLA Modules:
  0.0 83.6 jit_solution(6622850197661251026)
XLA Ops:
  0.0 81.9 %layer.1 = bf16[128,1280]{1,0:T(8,128)(2,1)} custom-call(s32[16]{0:T(128)} %lens.1, bf16[128,5120]{1,0:T(8,128)(2,1)} %hid.1, bf16[80,640]{1,0:T(8,128)(2,1)} %wq.1, bf16[80,256]{1,0:T(8,128)(2,1)} %bitcast.3, bf16[80,640]{1,0:T(8,128)(2,1)} %bitcast.2, f32[1,128]{1,0:T(1,128)} %constant.2.clone.freq), custom_call_target="tpu_custom_call" | custom-call | tf_op jit(solution)/shard_map/layer/pallas_call | solution.py:569
  81.9 1.7 %copy.8 = bf16[128,1280]{1,0:T(8,128)(2,1)} copy(bf16[128,1280]{1,0:T(8,128)(2,1)} %layer.1) | data formatting | bytes 655360

commit v4 on v3

--- a/solution.py
+++ b/solution.py
@@ -430,41 +430,41 @@
 
     c_hop(2)
     c_hop(-2)
+    c_hop(1)
     ring_e.hop(4)
     for r in (3, 7, 4, 8):
         project(ring_e, wqc, acc_r, rs, r, 384)
     for k in ORDER:
         r_copy(k).start()
-    c_hop(1)
     ring_d.start()
     c_plane(0)
     chunk(0, c, 0, init=True)
-    ring_d.hop(1)
     c_hop(3)
     c_hop(4)
+    ring_d.hop(1)
     c_other(0)
     chunk(0, 1 - c, 0)
     c_plane(1)
     c_plane(2)
     reach(1, c, (0,))
+    ring_d.hop(2)
     queries(acc_r, rr, r_copy, 2, 3)
     chunk(0, c, 1, init=True)
     chunk(0, 1 - c, 1)
-    ring_d.hop(2)
     reach(1, c, (1,))
+    ring_d.hop(3)
     c_other(1)
     reach(1, 1 - c)
     c_plane(3)
     c_plane(4)
     reach(2, c)
+    ring_d.hop(4)
     c_other(2)
     reach(2, 1 - c)
-    ring_d.hop(3)
     reach(3, c)
     reach(4, c)
     c_other(3)
     reach(3, 1 - c)
-    ring_d.hop(4)
     c_other(4)
     reach(4, 1 - c)
 

time: 83.7 us -> 82.2 us (0.982)
  Pallas kernels: 81.9 us -> 79.8 us
    pallas_call x1, Pallas kernels: 81.9 us -> 79.8 us  [local(): pl.pallas_call(kernel, out_shape=jax.ShapeDtypeStruct((ROWS, 1280), BF),...]
where the time goes in v4:
time: 82.2 us; the launch traced here: 81.5 us
  Pallas kernels  79.8 us (97%)
  local copies, waits for them, and re-layouts  1.72 us (2%)
    pallas_call x1, Pallas kernels, local(): pl.pallas_call(kernel, out_shape=jax.ShapeDtypeStruct((ROWS, 1280), BF),...  79.8 us
    unnamed x1, local copies, waits for them, and re-layouts  1.72 us

profile of v4, /device:TPU:1, one launch (start us, length us, event | category | flops | bytes accessed | tf_op | source)
XLA Modules:
  0.0 81.5 jit_solution(12525726576978185145)
XLA Ops:
  0.0 79.8 %layer.1 = bf16[128,1280]{1,0:T(8,128)(2,1)} custom-call(s32[16]{0:T(128)} %lens.1, bf16[128,5120]{1,0:T(8,128)(2,1)} %hid.1, bf16[80,640]{1,0:T(8,128)(2,1)} %wq.1, bf16[80,256]{1,0:T(8,128)(2,1)} %bitcast.3, bf16[80,640]{1,0:T(8,128)(2,1)} %bitcast.2, f32[1,128]{1,0:T(1,128)} %constant.2.clone.freq), custom_call_target="tpu_custom_call" | custom-call | tf_op jit(solution)/shard_map/layer/pallas_call | solution.py:569
  79.8 1.7 %copy.8 = bf16[128,1280]{1,0:T(8,128)(2,1)} copy(bf16[128,1280]{1,0:T(8,128)(2,1)} %layer.1) | data formatting | bytes 655360
